TPU v7x, 512 devices: a whole 4x4x16 slice. The times are simulated.
512 devices in a mesh: dp: 128 (over z, x, y_lo), sub: 4 (over y_hi, core).
Axes of the slice: x: 4, y: 4 (y_hi: 2, y_lo: 2; y = y_hi * 2 + y_lo), z: 16, core: 2. Of those that a mesh axis runs over, the one named last changes fastest.
Arguments:
- queries: bfloat16 [16384, 4096], P('dp', 'sub'), may hold values from -1 to 1
- passages: bfloat16 [768, 4096], P('dp', 'sub'), may hold values from -1 to 1
- positive_bank: bfloat16 [2048, 4096], P('dp', 'sub'), may hold values from -1 to 1
- positive_ids: int32 [16384, 16], P('dp'), may hold values from -1 to 2047, as said below
- positive_counts: int32 [16384], P('dp'), may hold values from 1 to 16
Outputs:
- losses: float32 [16384], P('dp')
- query_grad: float32 [16384, 4096], P('dp', 'sub')
- passage_grad: float32 [768, 4096], P('dp', 'sub')
- bank_grad: float32 [2048, 4096], P('dp', 'sub')
Inputs may be any that keep to these rules, and one draw needn't show every extreme that they name: `positive_ids`: entries of row i before position positive_counts[i] are rows of positive_bank, the rest are -1. The valid entries of the 128 queries of one index of dp name rows held by any one index of dp at most 2 times in all (repeats counted), a bound that is reached. In each aligned block of 16 queries at most one query has more than one valid entry.
All inputs are finite; a program needn't handle non-finite values.
Results may differ from a plain program's by a relative error of at most 0.0019.
Values may be sent and summed in bfloat16 or wider, within the bound.
A program may use at most 64 MiB of HBM per device.

v0:
```python
import jax
import jax.numpy as jnp
from jax import lax
from jax.sharding import PartitionSpec as P


def softmax_terms(score_sums, pos_sums, counts):
    scores = score_sums * 50.0
    pos_scores = pos_sums * 50.0
    is_valid = jnp.arange(pos_scores.shape[1])[None, :] < counts[:, None]
    row_max = jnp.maximum(jnp.max(scores, 1), jnp.max(jnp.where(is_valid, pos_scores, -jnp.inf), 1))
    row_total = jnp.sum(jnp.exp(scores - row_max[:, None]), 1)
    row_total = row_total + jnp.sum(
        jnp.exp(jnp.where(is_valid, pos_scores - row_max[:, None], -jnp.inf)), 1
    )
    log_total = row_max + jnp.log(row_total)
    inv_count = 1.0 / counts.astype(jnp.float32)
    query_loss = log_total - jnp.sum(jnp.where(is_valid, pos_scores, 0.0), 1) * inv_count
    weights = jnp.exp(scores - log_total[:, None]).astype(jnp.bfloat16)
    coeffs = jnp.where(
        is_valid,
        jnp.exp(jnp.where(is_valid, pos_scores - log_total[:, None], -jnp.inf))
        - inv_count[:, None],
        0.0,
    )
    return (query_loss, weights, coeffs)


def body(queries, passages, positive_bank, positive_ids, positive_counts):
    peer_count = lax.axis_size("dp")
    query_count, col_width = queries.shape
    bank_rows = positive_bank.shape[0]
    capacity = bank_rows // 8
    max_pos = positive_ids.shape[1]
    slot_total = peer_count * capacity
    flat_ids = positive_ids.reshape(-1)
    is_live = (jnp.arange(max_pos)[None, :] < positive_counts[:, None]).reshape(-1)
    owner_dev = jnp.where(is_live, flat_ids // bank_rows, 0)
    onehot = ((owner_dev[:, None] == jnp.arange(peer_count)[None, :]) & is_live[:, None]).astype(
        jnp.int32
    )
    slot_rank = jnp.sum(jnp.cumsum(onehot, 0) * onehot, 1) - 1
    slot_of = jnp.where(is_live, owner_dev * capacity + slot_rank, slot_total)
    local_ids = jnp.where(is_live, flat_ids % bank_rows, -1)
    send_ids = jnp.full((slot_total + 1,), -1, jnp.int32).at[slot_of].set(local_ids)[:slot_total]
    slot_request = (
        jnp.zeros((slot_total + 1,), jnp.int32)
        .at[slot_of]
        .set(jnp.arange(flat_ids.shape[0], dtype=jnp.int32))[:slot_total]
    )
    slot_live = send_ids >= 0
    slot_query = slot_request // max_pos
    wanted = lax.all_to_all(
        send_ids.reshape(peer_count, capacity), "dp", split_axis=0, concat_axis=0, tiled=True
    ).reshape(-1)
    served = wanted >= 0
    picked = jnp.where(
        served[:, None],
        positive_bank[jnp.clip(wanted, 0, bank_rows - 1)],
        jnp.zeros((), jnp.bfloat16),
    )
    fetched = lax.all_to_all(
        picked.reshape(peer_count, capacity, col_width),
        "dp",
        split_axis=0,
        concat_axis=0,
        tiled=True,
    ).reshape(slot_total, col_width)
    query_slots = queries[slot_query]
    slot_scores = jnp.einsum("sd,sd->s", query_slots, fetched, preferred_element_type=jnp.float32)
    pos_part = jnp.concatenate([slot_scores, jnp.zeros((1,), jnp.float32)])[slot_of].reshape(
        query_count, max_pos
    )
    all_passages = lax.all_gather(passages, "dp", axis=0, tiled=True)
    score_part = lax.dot_general(
        queries, all_passages, (((1,), (1,)), ((), ())), preferred_element_type=jnp.float32
    )
    score_sums, pos_sums = lax.psum((score_part, pos_part), "sub")
    losses, weights, coeffs = softmax_terms(score_sums, pos_sums, positive_counts)
    slot_coeff = jnp.where(slot_live, coeffs.reshape(-1)[slot_request], 0.0)
    pos_grad = jax.ops.segment_sum(
        slot_coeff[:, None] * fetched.astype(jnp.float32), slot_query, query_count
    )
    query_grad = 50.0 * (
        jnp.dot(weights, all_passages, preferred_element_type=jnp.float32) + pos_grad
    )
    passage_grad = 50.0 * lax.psum_scatter(
        lax.dot_general(
            weights, queries, (((0,), (0,)), ((), ())), preferred_element_type=jnp.float32
        ),
        "dp",
        scatter_dimension=0,
        tiled=True,
    )
    grad_rows = (slot_coeff[:, None] * query_slots.astype(jnp.float32)).reshape(
        peer_count, capacity, col_width
    )
    bank_terms = lax.all_to_all(grad_rows, "dp", split_axis=0, concat_axis=0, tiled=True).reshape(
        slot_total, col_width
    )
    member = (
        jnp.where(served, wanted, bank_rows)[None, :] == jnp.arange(bank_rows)[:, None]
    ).astype(jnp.float32)
    bank_grad = 50.0 * jnp.dot(member, bank_terms, precision=lax.Precision.HIGHEST)
    return (losses, query_grad, passage_grad, bank_grad)


def solution(mesh):
    placed = (P("dp", "sub"), P("dp", "sub"), P("dp", "sub"), P("dp", None), P("dp"))
    return jax.shard_map(
        body,
        mesh=mesh,
        in_specs=placed,
        out_specs=(P("dp"), P("dp", "sub"), P("dp", "sub"), P("dp", "sub")),
        check_vma=False,
    )
```

profile of v0, /device:TPU:2, one launch (start us, length us, event | category | flops | bytes accessed | tf_op | source)
XLA Modules:
  0.0 1186.1 jit_solution(14348177609646131720)
XLA Ops:
  13.5 8.0 scatter_custom_fusion.1
  21.7 34.5 %all_to_all.19 = s32[128,1,2]{2,1,0:T(1,128)S(1)} all-to-all(s32[128,1,2]{2,1,0:T(1,128)S(1)} %bitcast.24), channel_id=1, replica_groups=mesh['dp'=128,'sub'=4] {'dp'}, dimensions={0} | all-to-all | bytes 2048 | tf_op jit(solution)/shard_map/all_to_all | solution.py:53
  61.0 6.6 all-to-all-start.1
  67.7 8.2 scatter_custom_fusion
  79.3 18.1 %all-to-all-done.1 = bf16[128,2,1024]{2,1,0:T(2,128)(2,1)S(1)} async-done(((bf16[128,2,1024]{2,1,0:T(2,128)(2,1)}), bf16[128,2,1024]{2,1,0:T(2,128)(2,1)S(1)}, u32[]{:S(2)}, u32[]{:S(2)}) %all-to-all-start.1) | async-done | bytes 524320 | tf_op jit(solution)/shard_map/all_to_all | solution.py:62
  97.7 505.5 %all-gather.3.cloned.1.call-done = bf16[128,6,1024]{2,1,0:T(8,128)(2,1)} async-done(((bf16[1,6,1024]{2,1,0:T(8,128)(2,1)}), bf16[128,6,1024]{2,1,0:T(8,128)(2,1)}) %all-gather.3.cloned.1.call-update) | async-done | bytes 1572880 | tf_op jit(solution)/shard_map/all_gather | solution.py:74
  603.2 2.6 reshape.365
  607.5 13.2 %gather_fusion.2 = f32[2048]{0:T(1024)S(1)} fusion(f32[257]{0:T(512)S(1)} %pad_maximum_fusion, s32[2048]{0:T(1024)S(1)} %broadcast_clamp_fusion), kind=kCustom, calls=%fused_computation.2 | custom fusion | bytes 24576 | tf_op jit(solution)/shard_map/gather | solution.py:71
  621.4 14.3 %psum.15 = f32[128,16]{1,0:T(8,128)S(1)} all-reduce(f32[128,16]{1,0:T(8,128)} %reshape.300), channel_id=1, replica_groups=mesh['dp'=128,'sub'=4] {'sub'}, use_global_device_ids=true, to_apply=%region_7.8 | all-reduce | flops 2048 | bytes 16384 | tf_op jit(solution)/shard_map/psum | solution.py:78
  635.9 26.8 %all-reduce.4.cloned.1.call-done = f32[128,768]{1,0:T(8,128)} async-done(((f32[128,768]{1,0:T(8,128)}), f32[128,768]{1,0:T(8,128)}) %all-reduce.4.cloned.1.call-update) | async-done | bytes 393232 | tf_op jit(solution)/shard_map/psum | solution.py:78
  670.8 17.1 %all-to-all-start.2 = ((f32[128,2,1024]{2,1,0:T(2,128)}), f32[128,2,1024]{2,1,0:T(2,128)}, u32[]{:S(2)}, u32[]{:S(2)}) async-start(f32[128,2,1024]{2,1,0:T(2,128)} %broadcast_multiply_fusion), calls=%async_computation.2 | async-start | bytes 2097152 | tf_op jit(solution)/shard_map/all_to_all | solution.py:98
  690.3 360.5 %fusion = f32[8,1024]{1,0:T(8,128)S(1)} fusion(f32[768,1024]{1,0:T(8,128)} %fusion.24), kind=kCustom, calls=%all-reduce-scatter | all-reduce-scatter fusion | flops 1048577 | bytes 3180544
  1050.8 12.1 %collective-permute-start.30 = (f32[8,1024]{1,0:T(8,128)S(1)}, f32[8,1024]{1,0:T(8,128)S(1)}, u32[]{:S(2)}, u32[]{:S(2)}) collective-permute-start(f32[8,1024]{1,0:T(8,128)S(1)} %fusion), channel_id=1, source_target_pairs={{0,124},{4,128},{8,132},{12,136},{16,140},{20,144},{24,148},{28,15... | collective-permute-start | bytes 98312
  1063.0 6.6 collective-permute-start.31
  1069.5 5.5 collective-permute-start.29
  1082.9 8.7 collective-permute-start.22
  1091.6 6.9 collective-permute-start.21
  1104.6 2.8 collective-permute-start.17
  1107.4 5.7 collective-permute-start.16
  1120.6 3.1 collective-permute-start.12
  1123.8 3.8 collective-permute-start.11
  1127.6 2.5 collective-permute-start.10
  1130.2 3.4 collective-permute-start.9
  1133.5 2.8 collective-permute-start.8
  1138.6 2.8 collective-permute-start.6
  1142.2 3.2 collective-permute-start.5
  1145.9 3.1 scatter_custom_fusion.2
  1149.1 2.5 collective-permute-start.4
  1154.0 4.3 collective-permute-start.2
  1158.4 3.1 collective-permute-start.1
  1161.5 3.6 collective-permute-start
  1168.3 7.3 concatenate.4
  (193 shorter events, 60.9 us)
Async XLA Ops:
  7.2 596.0 %all-gather.3.cloned.1.call-start = ((), (), s32[]{:S(2)}) async-start(), calls=%async_computation.4 | async-start | bytes 2113536 | tf_op jit(solution)/shard_map/all_gather | solution.py:74
  61.0 36.4 %all-to-all-start.1 = ((bf16[128,2,1024]{2,1,0:T(2,128)(2,1)}), bf16[128,2,1024]{2,1,0:T(2,128)(2,1)S(1)}, u32[]{:S(2)}, u32[]{:S(2)}) async-start(bf16[128,2,1024]{2,1,0:T(2,128)(2,1)} %broadcast_select_fusion), calls=%async_computation.1 | async-start | bytes 1048576 | tf_op jit(solution)/shard_map/all_to_all | solution.py:62
  67.6 595.1 %all-reduce.4.cloned.1.call-start = ((), (), s32[]{:S(2)}) async-start(), calls=%async_computation.3 | async-start | bytes 786432 | tf_op jit(solution)/shard_map/psum | solution.py:78
  670.8 505.4 %all-to-all-start.2 = ((f32[128,2,1024]{2,1,0:T(2,128)}), f32[128,2,1024]{2,1,0:T(2,128)}, u32[]{:S(2)}, u32[]{:S(2)}) async-start(f32[128,2,1024]{2,1,0:T(2,128)} %broadcast_multiply_fusion), calls=%async_computation.2 | async-start | bytes 2097152 | tf_op jit(solution)/shard_map/all_to_all | solution.py:98
  1050.8 28.1 %collective-permute-start.30 = (f32[8,1024]{1,0:T(8,128)S(1)}, f32[8,1024]{1,0:T(8,128)S(1)}, u32[]{:S(2)}, u32[]{:S(2)}) collective-permute-start(f32[8,1024]{1,0:T(8,128)S(1)} %fusion), channel_id=1, source_target_pairs={{0,124},{4,128},{8,132},{12,136},{16,140},{20,144},{24,148},{28,15... | collective-permute-start | bytes 98312
  1063.0 14.7 %collective-permute-start.31 = (f32[6,1024]{1,0:T(8,128)S(1)}, f32[6,1024]{1,0:T(8,128)S(1)}, u32[]{:S(2)}, u32[]{:S(2)}) collective-permute-start(f32[6,1024]{1,0:T(8,128)S(1)} %slice.26), channel_id=1, source_target_pairs={{0,128},{4,132},{8,136},{12,140},{16,144},{20,148},{24,152},{28,15... | collective-permute-start | bytes 73736
  1069.5 10.7 collective-permute-start.29
  1077.6 14.0 %collective-permute-start.26 = (f32[8,1024]{1,0:T(8,128)S(1)}, f32[8,1024]{1,0:T(8,128)S(1)}, u32[]{:S(2)}, u32[]{:S(2)}) collective-permute-start(f32[8,1024]{1,0:T(8,128)S(1)} %fusion), channel_id=1, source_target_pairs={{0,108},{4,112},{8,116},{12,120},{16,124},{20,128},{24,132},{28,13... | collective-permute-start | bytes 98312
  1078.9 19.6 %collective-permute-start.25 = (f32[8,1024]{1,0:T(8,128)S(1)}, f32[8,1024]{1,0:T(8,128)S(1)}, u32[]{:S(2)}, u32[]{:S(2)}) collective-permute-start(f32[8,1024]{1,0:T(8,128)S(1)} %fusion), channel_id=1, source_target_pairs={{0,104},{4,108},{8,112},{12,116},{16,120},{20,124},{24,128},{28,13... | collective-permute-start | bytes 98312
  1080.2 20.6 %collective-permute-start.24 = (f32[8,1024]{1,0:T(8,128)S(1)}, f32[8,1024]{1,0:T(8,128)S(1)}, u32[]{:S(2)}, u32[]{:S(2)}) collective-permute-start(f32[8,1024]{1,0:T(8,128)S(1)} %fusion), channel_id=1, source_target_pairs={{0,100},{4,104},{8,108},{12,112},{16,116},{20,120},{24,124},{28,12... | collective-permute-start | bytes 98312
  1081.5 21.7 %collective-permute-start.23 = (f32[8,1024]{1,0:T(8,128)S(1)}, f32[8,1024]{1,0:T(8,128)S(1)}, u32[]{:S(2)}, u32[]{:S(2)}) collective-permute-start(f32[8,1024]{1,0:T(8,128)S(1)} %fusion), channel_id=1, source_target_pairs={{0,96},{4,100},{8,104},{12,108},{16,112},{20,116},{24,120},{28,124... | collective-permute-start | bytes 98312
  1082.9 21.7 %collective-permute-start.22 = (f32[8,1024]{1,0:T(8,128)S(1)}, f32[8,1024]{1,0:T(8,128)S(1)}, u32[]{:S(2)}, u32[]{:S(2)}) collective-permute-start(f32[8,1024]{1,0:T(8,128)S(1)} %fusion), channel_id=1, source_target_pairs={{0,92},{4,96},{8,100},{12,104},{16,108},{20,112},{24,116},{28,120}... | collective-permute-start | bytes 98312
  1091.6 15.7 %collective-permute-start.21 = (f32[8,1024]{1,0:T(8,128)S(1)}, f32[8,1024]{1,0:T(8,128)S(1)}, u32[]{:S(2)}, u32[]{:S(2)}) collective-permute-start(f32[8,1024]{1,0:T(8,128)S(1)} %fusion), channel_id=1, source_target_pairs={{0,88},{4,92},{8,96},{12,100},{16,104},{20,108},{24,112},{28,116},... | collective-permute-start | bytes 98312
  1098.6 14.5 %collective-permute-start.20 = (f32[8,1024]{1,0:T(8,128)S(1)}, f32[8,1024]{1,0:T(8,128)S(1)}, u32[]{:S(2)}, u32[]{:S(2)}) collective-permute-start(f32[8,1024]{1,0:T(8,128)S(1)} %fusion), channel_id=1, source_target_pairs={{0,84},{4,88},{8,92},{12,96},{16,100},{20,104},{24,108},{28,112},{... | collective-permute-start | bytes 98312
  1100.8 15.6 %collective-permute-start.19 = (f32[8,1024]{1,0:T(8,128)S(1)}, f32[8,1024]{1,0:T(8,128)S(1)}, u32[]{:S(2)}, u32[]{:S(2)}) collective-permute-start(f32[8,1024]{1,0:T(8,128)S(1)} %fusion), channel_id=1, source_target_pairs={{0,80},{4,84},{8,88},{12,92},{16,96},{20,100},{24,104},{28,108},{3... | collective-permute-start | bytes 98312
  1103.3 15.2 %collective-permute-start.18 = (f32[8,1024]{1,0:T(8,128)S(1)}, f32[8,1024]{1,0:T(8,128)S(1)}, u32[]{:S(2)}, u32[]{:S(2)}) collective-permute-start(f32[8,1024]{1,0:T(8,128)S(1)} %fusion), channel_id=1, source_target_pairs={{0,76},{4,80},{8,84},{12,88},{16,92},{20,96},{24,100},{28,104},{32... | collective-permute-start | bytes 98312
  1104.6 16.0 %collective-permute-start.17 = (f32[8,1024]{1,0:T(8,128)S(1)}, f32[8,1024]{1,0:T(8,128)S(1)}, u32[]{:S(2)}, u32[]{:S(2)}) collective-permute-start(f32[8,1024]{1,0:T(8,128)S(1)} %fusion), channel_id=1, source_target_pairs={{0,72},{4,76},{8,80},{12,84},{16,88},{20,92},{24,96},{28,100},{32,... | collective-permute-start | bytes 98312
  1107.4 16.4 %collective-permute-start.16 = (f32[8,1024]{1,0:T(8,128)S(1)}, f32[8,1024]{1,0:T(8,128)S(1)}, u32[]{:S(2)}, u32[]{:S(2)}) collective-permute-start(f32[8,1024]{1,0:T(8,128)S(1)} %fusion), channel_id=1, source_target_pairs={{0,68},{4,72},{8,76},{12,80},{16,84},{20,88},{24,92},{28,96},{32,1... | collective-permute-start | bytes 98312
  1113.1 14.5 %collective-permute-start.15 = (f32[8,1024]{1,0:T(8,128)S(1)}, f32[8,1024]{1,0:T(8,128)S(1)}, u32[]{:S(2)}, u32[]{:S(2)}) collective-permute-start(f32[8,1024]{1,0:T(8,128)S(1)} %fusion), channel_id=1, source_target_pairs={{0,64},{4,68},{8,72},{12,76},{16,80},{20,84},{24,88},{28,92},{32,9... | collective-permute-start | bytes 98312
  1116.5 13.7 %collective-permute-start.14 = (f32[8,1024]{1,0:T(8,128)S(1)}, f32[8,1024]{1,0:T(8,128)S(1)}, u32[]{:S(2)}, u32[]{:S(2)}) collective-permute-start(f32[8,1024]{1,0:T(8,128)S(1)} %fusion), channel_id=1, source_target_pairs={{0,60},{4,64},{8,68},{12,72},{16,76},{20,80},{24,84},{28,88},{32,9... | collective-permute-start | bytes 98312
  1118.5 15.0 %collective-permute-start.13 = (f32[8,1024]{1,0:T(8,128)S(1)}, f32[8,1024]{1,0:T(8,128)S(1)}, u32[]{:S(2)}, u32[]{:S(2)}) collective-permute-start(f32[8,1024]{1,0:T(8,128)S(1)} %fusion), channel_id=1, source_target_pairs={{0,56},{4,60},{8,64},{12,68},{16,72},{20,76},{24,80},{28,84},{32,8... | collective-permute-start | bytes 98312
  1120.6 15.8 %collective-permute-start.12 = (f32[8,1024]{1,0:T(8,128)S(1)}, f32[8,1024]{1,0:T(8,128)S(1)}, u32[]{:S(2)}, u32[]{:S(2)}) collective-permute-start(f32[8,1024]{1,0:T(8,128)S(1)} %fusion), channel_id=1, source_target_pairs={{0,52},{4,56},{8,60},{12,64},{16,68},{20,72},{24,76},{28,80},{32,8... | collective-permute-start | bytes 98312
  1123.8 14.8 %collective-permute-start.11 = (f32[8,1024]{1,0:T(8,128)S(1)}, f32[8,1024]{1,0:T(8,128)S(1)}, u32[]{:S(2)}, u32[]{:S(2)}) collective-permute-start(f32[8,1024]{1,0:T(8,128)S(1)} %fusion), channel_id=1, source_target_pairs={{0,48},{4,52},{8,56},{12,60},{16,64},{20,68},{24,72},{28,76},{32,8... | collective-permute-start | bytes 98312
  1127.6 13.8 %collective-permute-start.10 = (f32[8,1024]{1,0:T(8,128)S(1)}, f32[8,1024]{1,0:T(8,128)S(1)}, u32[]{:S(2)}, u32[]{:S(2)}) collective-permute-start(f32[8,1024]{1,0:T(8,128)S(1)} %fusion), channel_id=1, source_target_pairs={{0,44},{4,48},{8,52},{12,56},{16,60},{20,64},{24,68},{28,72},{32,7... | collective-permute-start | bytes 98312
  1130.2 18.9 %collective-permute-start.9 = (f32[8,1024]{1,0:T(8,128)S(1)}, f32[8,1024]{1,0:T(8,128)}, u32[]{:S(2)}, u32[]{:S(2)}) collective-permute-start(f32[8,1024]{1,0:T(8,128)S(1)} %fusion), channel_id=1, source_target_pairs={{0,40},{4,44},{8,48},{12,52},{16,56},{20,60},{24,64},{28,68},{32,7... | collective-permute-start | bytes 98312
  1133.5 18.0 %collective-permute-start.8 = (f32[8,1024]{1,0:T(8,128)S(1)}, f32[8,1024]{1,0:T(8,128)}, u32[]{:S(2)}, u32[]{:S(2)}) collective-permute-start(f32[8,1024]{1,0:T(8,128)S(1)} %fusion), channel_id=1, source_target_pairs={{0,36},{4,40},{8,44},{12,48},{16,52},{20,56},{24,60},{28,64},{32,6... | collective-permute-start | bytes 98312
  1136.4 17.6 %collective-permute-start.7 = (f32[8,1024]{1,0:T(8,128)S(1)}, f32[8,1024]{1,0:T(8,128)}, u32[]{:S(2)}, u32[]{:S(2)}) collective-permute-start(f32[8,1024]{1,0:T(8,128)S(1)} %fusion), channel_id=1, source_target_pairs={{0,32},{4,36},{8,40},{12,44},{16,48},{20,52},{24,56},{28,60},{32,6... | collective-permute-start | bytes 98312
  1138.6 19.8 %collective-permute-start.6 = (f32[8,1024]{1,0:T(8,128)S(1)}, f32[8,1024]{1,0:T(8,128)}, u32[]{:S(2)}, u32[]{:S(2)}) collective-permute-start(f32[8,1024]{1,0:T(8,128)S(1)} %fusion), channel_id=1, source_target_pairs={{0,28},{4,32},{8,36},{12,40},{16,44},{20,48},{24,52},{28,56},{32,6... | collective-permute-start | bytes 98312
  1142.2 19.3 %collective-permute-start.5 = (f32[8,1024]{1,0:T(8,128)S(1)}, f32[8,1024]{1,0:T(8,128)}, u32[]{:S(2)}, u32[]{:S(2)}) collective-permute-start(f32[8,1024]{1,0:T(8,128)S(1)} %fusion), channel_id=1, source_target_pairs={{0,24},{4,28},{8,32},{12,36},{16,40},{20,44},{24,48},{28,52},{32,5... | collective-permute-start | bytes 98312
  1149.1 16.9 %collective-permute-start.4 = (f32[8,1024]{1,0:T(8,128)S(1)}, f32[8,1024]{1,0:T(8,128)S(1)}, u32[]{:S(2)}, u32[]{:S(2)}) collective-permute-start(f32[8,1024]{1,0:T(8,128)S(1)} %fusion), channel_id=1, source_target_pairs={{0,20},{4,24},{8,28},{12,32},{16,36},{20,40},{24,44},{28,48},{32,5... | collective-permute-start | bytes 98312
  1151.6 14.4 %collective-permute-start.3 = (f32[8,1024]{1,0:T(8,128)S(1)}, f32[8,1024]{1,0:T(8,128)S(1)}, u32[]{:S(2)}, u32[]{:S(2)}) collective-permute-start(f32[8,1024]{1,0:T(8,128)S(1)} %fusion), channel_id=1, source_target_pairs={{0,16},{4,20},{8,24},{12,28},{16,32},{20,36},{24,40},{28,44},{32,4... | collective-permute-start | bytes 98312
  1154.0 11.9 %collective-permute-start.2 = (f32[8,1024]{1,0:T(8,128)S(1)}, f32[8,1024]{1,0:T(8,128)S(1)}, u32[]{:S(2)}, u32[]{:S(2)}) collective-permute-start(f32[8,1024]{1,0:T(8,128)S(1)} %fusion), channel_id=1, source_target_pairs={{0,12},{4,16},{8,20},{12,24},{16,28},{20,32},{24,36},{28,40},{32,4... | collective-permute-start | bytes 98312
  (39 other events, 953.2 us)
Sparse Core Ops, SparseCore 0:
  10.1 593.0 all-gather.2
  607.4 55.3 all-reduce.3
where the time goes:
time: 1190 us
  waiting for transfers between devices  554 us (47%)
  blocking collectives  409 us (34%)
  starting transfers between devices  131 us (11%)
  local copies, waits for them, and re-layouts  55.2 us (5%)
  other arithmetic  16.1 us (1%)
  between operations  15.9 us (1%)
    all_gather x1, waiting for transfers between devices, body(): all_passages = lax.all_gather(passages, 'dp', axis=0, tiled=True)  506 us
    unnamed x1, blocking collectives  361 us
    unnamed x32, starting transfers between devices  107 us
    all_to_all x1, blocking collectives, body(): lax.all_to_all(send_ids.reshape(peer_count, capacity), 'dp', split_axis=0...  34.5 us
    psum x1, waiting for transfers between devices, body(): score_sums, pos_sums = lax.psum((score_part, pos_part), 'sub')  26.8 us
  transfers between devices with their start and end apart: 36, of which 4 were waited for; matrix products, arithmetic and copies ran while one was open for 35% of the time, Pallas kernels for 0%

commit v1 on v0

--- a/solution.py
+++ b/solution.py
@@ -71,7 +71,9 @@
     pos_part = jnp.concatenate([slot_scores, jnp.zeros((1,), jnp.float32)])[slot_of].reshape(
         query_count, max_pos
     )
-    all_passages = lax.all_gather(passages, "dp", axis=0, tiled=True)
+    all_passages = jnp.concatenate(
+        lax.all_to_all(jnp.stack([passages] * lax.axis_size("dp")), "dp", 0, 0), axis=0
+    )
     score_part = lax.dot_general(
         queries, all_passages, (((1,), (1,)), ((), ())), preferred_element_type=jnp.float32
     )

time: 1190 us -> 783 us (0.66)
  waiting for transfers between devices: 554 us -> 109 us
  blocking collectives: 409 us -> 445 us
    all_gather x1 -> x0, waiting for transfers between devices: 506 us -> none  [body(): all_passages = lax.all_gather(passages, 'dp', axis=0, tiled=True)]
    all_to_all x1, waiting for transfers between devices: 18.1 us -> 80.6 us  [body(): lax.all_to_all(jnp.stack([passages] * lax.axis_size('dp')), 'dp', 0, 0)]
    all_to_all x0 -> x1, blocking collectives: none -> 35.9 us  [body(): lax.all_to_all(picked.reshape(peer_count, capacity, col_width), 'dp', spl...]
  transfers between devices with their start and end apart: 36 -> 35, of which waited for: 4 -> 3; matrix products, arithmetic and copies ran while one was open for 35% -> 52% of each run, Pallas kernels for 0% -> 0%
where the time goes in v1:
time: 783 us; the launch traced here: 781 us
  blocking collectives  445 us (57%)
  starting transfers between devices  134 us (17%)
  waiting for transfers between devices  109 us (14%)
  local copies, waits for them, and re-layouts  56.6 us (7%)
  between operations  16 us (2%)
  other arithmetic  15.5 us (2%)
    unnamed x1, blocking collectives  361 us
    unnamed x32, starting transfers between devices  107 us
    all_to_all x1, waiting for transfers between devices, body(): lax.all_to_all(jnp.stack([passages] * lax.axis_size('dp')), 'dp', 0, 0)  80.6 us
    all_to_all x1, blocking collectives, body(): lax.all_to_all(picked.reshape(peer_count, capacity, col_width), 'dp', spl...  35.9 us
    all_to_all x1, blocking collectives, body(): lax.all_to_all(send_ids.reshape(peer_count, capacity), 'dp', split_axis=0...  34.4 us
    psum x1, waiting for transfers between devices, body(): score_sums, pos_sums = lax.psum((score_part, pos_part), 'sub')  25.6 us
    all_to_all x1, starting transfers between devices, body(): lax.all_to_all(grad_rows, 'dp', split_axis=0, concat_axis=0, tiled=True)  17.1 us
  transfers between devices with their start and end apart: 35, of which 3 were waited for; matrix products, arithmetic and copies ran while one was open for 52% of the time, Pallas kernels for 0%

profile of v1, /device:TPU:2, one launch (start us, length us, event | category | flops | bytes accessed | tf_op | source)
XLA Modules:
  0.0 780.9 jit_solution(15012784337791566148)
XLA Ops:
  12.9 8.0 %scatter_custom_fusion.1 = s32[257]{0:T(512)S(1)} fusion(s32[2048]{0:T(1024)S(1)} %bitcast.22, s32[2048]{0:T(1024)S(1)} %get-tuple-element.15, s32[]{:T(128)} %constant.39.clone.1), kind=kCustom, calls=%fused_computation.79 | custom fusion | bytes 1032 | tf_op jit(solution)/shard_map/scatter | solution.py:45
  21.1 34.4 %all_to_all.24 = s32[128,1,2]{2,1,0:T(1,128)S(1)} all-to-all(s32[128,1,2]{2,1,0:T(1,128)S(1)} %bitcast.21), channel_id=1, replica_groups=mesh['dp'=128,'sub'=4] {'dp'}, dimensions={0} | all-to-all | bytes 2048 | tf_op jit(solution)/shard_map/all_to_all | solution.py:53
  59.5 35.9 %all_to_all.25 = bf16[128,2,1024]{2,1,0:T(2,128)(2,1)S(1)} all-to-all(bf16[128,2,1024]{2,1,0:T(2,128)(2,1)S(1)} %broadcast_select_fusion), channel_id=1, replica_groups=mesh['dp'=128,'sub'=4] {'dp'}, dimensions={0} | all-to-all | bytes 1048576 | tf_op jit(solution)/shard_map/all_to_all | solution.py:62
  96.9 9.6 %all-to-all-start = ((bf16[128,6,1024]{2,1,0:T(8,128)(2,1)}), bf16[128,6,1024]{2,1,0:T(8,128)(2,1)}, u32[]{:S(2)}, u32[]{:S(2)}) async-start(bf16[128,6,1024]{2,1,0:T(8,128)(2,1)} %stack.2), calls=%async_computation | async-start | bytes 4194304 | tf_op jit(solution)/shard_map/all_to_all | solution.py:75
  106.8 8.0 %scatter_custom_fusion = s32[257]{0:T(512)S(1)} fusion(s32[2048]{0:T(1024)S(1)} %bitcast.23, s32[2048]{0:T(1024)S(1)} %iota.22, s32[]{:T(128)} %constant.32.clone.1), kind=kCustom, calls=%fused_computation.81 | custom fusion | bytes 1032 | tf_op jit(solution)/shard_map/scatter | solution.py:49
  118.4 80.6 %all-to-all-done = bf16[128,6,1024]{2,1,0:T(8,128)(2,1)} async-done(((bf16[128,6,1024]{2,1,0:T(8,128)(2,1)}), bf16[128,6,1024]{2,1,0:T(8,128)(2,1)}, u32[]{:S(2)}, u32[]{:S(2)}) %all-to-all-start) | async-done | bytes 1572896 | tf_op jit(solution)/shard_map/all_to_all | solution.py:75
  199.0 2.6 reshape.300
  203.3 13.2 %gather_fusion.2 = f32[2048]{0:T(1024)S(1)} fusion(f32[257]{0:T(512)S(1)} %pad_maximum_fusion, s32[2048]{0:T(1024)S(1)} %broadcast_clamp_fusion), kind=kCustom, calls=%fused_computation.2 | custom fusion | bytes 24576 | tf_op jit(solution)/shard_map/gather | solution.py:71
  217.2 14.2 %psum.15 = f32[128,16]{1,0:T(8,128)S(1)} all-reduce(f32[128,16]{1,0:T(8,128)} %reshape.306), channel_id=1, replica_groups=mesh['dp'=128,'sub'=4] {'sub'}, use_global_device_ids=true, to_apply=%region_7.8 | all-reduce | flops 2048 | bytes 16384 | tf_op jit(solution)/shard_map/psum | solution.py:80
  231.6 25.6 %all-reduce.4.cloned.1.call-done = f32[128,768]{1,0:T(8,128)} async-done(((f32[128,768]{1,0:T(8,128)}), f32[128,768]{1,0:T(8,128)}) %all-reduce.4.cloned.1.call-update) | async-done | bytes 393232 | tf_op jit(solution)/shard_map/psum | solution.py:80
  265.2 17.1 %all-to-all-start.3 = ((f32[128,2,1024]{2,1,0:T(2,128)}), f32[128,2,1024]{2,1,0:T(2,128)}, u32[]{:S(2)}, u32[]{:S(2)}) async-start(f32[128,2,1024]{2,1,0:T(2,128)} %broadcast_multiply_fusion), calls=%async_computation.3 | async-start | bytes 2097152 | tf_op jit(solution)/shard_map/all_to_all | solution.py:100
  284.7 360.5 %fusion = f32[8,1024]{1,0:T(8,128)S(1)} fusion(f32[768,1024]{1,0:T(8,128)} %fusion.24), kind=kCustom, calls=%all-reduce-scatter | all-reduce-scatter fusion | flops 1048577 | bytes 3180544
  645.2 12.1 %collective-permute-start.30 = (f32[8,1024]{1,0:T(8,128)S(1)}, f32[8,1024]{1,0:T(8,128)S(1)}, u32[]{:S(2)}, u32[]{:S(2)}) collective-permute-start(f32[8,1024]{1,0:T(8,128)S(1)} %fusion), channel_id=1, source_target_pairs={{0,124},{4,128},{8,132},{12,136},{16,140},{20,144},{24,148},{28,15... | collective-permute-start | bytes 98312
  657.4 6.6 collective-permute-start.31
  663.9 5.5 collective-permute-start.29
  677.3 8.8 %collective-permute-start.22 = (f32[8,1024]{1,0:T(8,128)S(1)}, f32[8,1024]{1,0:T(8,128)S(1)}, u32[]{:S(2)}, u32[]{:S(2)}) collective-permute-start(f32[8,1024]{1,0:T(8,128)S(1)} %fusion), channel_id=1, source_target_pairs={{0,92},{4,96},{8,100},{12,104},{16,108},{20,112},{24,116},{28,120}... | collective-permute-start | bytes 98312
  686.1 6.9 collective-permute-start.21
  699.0 3.0 collective-permute-start.17
  702.0 5.4 collective-permute-start.16
  714.7 3.5 collective-permute-start.12
  718.2 3.8 collective-permute-start.11
  722.0 2.5 collective-permute-start.10
  724.6 3.4 collective-permute-start.9
  728.0 2.8 collective-permute-start.8
  733.0 2.8 collective-permute-start.6
  736.6 3.2 collective-permute-start.5
  740.4 3.3 scatter_custom_fusion.2
  743.8 2.5 collective-permute-start.4
  748.7 4.4 collective-permute-start.2
  753.1 3.1 collective-permute-start.1
  756.2 3.4 collective-permute-start
  763.1 7.3 concatenate.4
  (202 shorter events, 61.0 us)
Async XLA Ops:
  96.9 102.1 %all-to-all-start = ((bf16[128,6,1024]{2,1,0:T(8,128)(2,1)}), bf16[128,6,1024]{2,1,0:T(8,128)(2,1)}, u32[]{:S(2)}, u32[]{:S(2)}) async-start(bf16[128,6,1024]{2,1,0:T(8,128)(2,1)} %stack.2), calls=%async_computation | async-start | bytes 4194304 | tf_op jit(solution)/shard_map/all_to_all | solution.py:75
  106.5 150.6 %all-reduce.4.cloned.1.call-start = ((), (), s32[]{:S(2)}) async-start(), calls=%async_computation.4 | async-start | bytes 786432 | tf_op jit(solution)/shard_map/psum | solution.py:80
  265.2 505.8 %all-to-all-start.3 = ((f32[128,2,1024]{2,1,0:T(2,128)}), f32[128,2,1024]{2,1,0:T(2,128)}, u32[]{:S(2)}, u32[]{:S(2)}) async-start(f32[128,2,1024]{2,1,0:T(2,128)} %broadcast_multiply_fusion), calls=%async_computation.3 | async-start | bytes 2097152 | tf_op jit(solution)/shard_map/all_to_all | solution.py:100
  645.2 28.1 %collective-permute-start.30 = (f32[8,1024]{1,0:T(8,128)S(1)}, f32[8,1024]{1,0:T(8,128)S(1)}, u32[]{:S(2)}, u32[]{:S(2)}) collective-permute-start(f32[8,1024]{1,0:T(8,128)S(1)} %fusion), channel_id=1, source_target_pairs={{0,124},{4,128},{8,132},{12,136},{16,140},{20,144},{24,148},{28,15... | collective-permute-start | bytes 98312
  657.4 14.7 %collective-permute-start.31 = (f32[6,1024]{1,0:T(8,128)S(1)}, f32[6,1024]{1,0:T(8,128)S(1)}, u32[]{:S(2)}, u32[]{:S(2)}) collective-permute-start(f32[6,1024]{1,0:T(8,128)S(1)} %slice.26), channel_id=1, source_target_pairs={{0,128},{4,132},{8,136},{12,140},{16,144},{20,148},{24,152},{28,15... | collective-permute-start | bytes 73736
  663.9 10.7 %collective-permute-start.29 = (f32[8,1024]{1,0:T(8,128)S(1)}, f32[8,1024]{1,0:T(8,128)S(1)}, u32[]{:S(2)}, u32[]{:S(2)}) collective-permute-start(f32[8,1024]{1,0:T(8,128)S(1)} %fusion), channel_id=1, source_target_pairs={{0,120},{4,124},{8,128},{12,132},{16,136},{20,140},{24,144},{28,14... | collective-permute-start | bytes 98312
  672.0 14.0 %collective-permute-start.26 = (f32[8,1024]{1,0:T(8,128)S(1)}, f32[8,1024]{1,0:T(8,128)S(1)}, u32[]{:S(2)}, u32[]{:S(2)}) collective-permute-start(f32[8,1024]{1,0:T(8,128)S(1)} %fusion), channel_id=1, source_target_pairs={{0,108},{4,112},{8,116},{12,120},{16,124},{20,128},{24,132},{28,13... | collective-permute-start | bytes 98312
  673.3 19.6 %collective-permute-start.25 = (f32[8,1024]{1,0:T(8,128)S(1)}, f32[8,1024]{1,0:T(8,128)S(1)}, u32[]{:S(2)}, u32[]{:S(2)}) collective-permute-start(f32[8,1024]{1,0:T(8,128)S(1)} %fusion), channel_id=1, source_target_pairs={{0,104},{4,108},{8,112},{12,116},{16,120},{20,124},{24,128},{28,13... | collective-permute-start | bytes 98312
  674.7 20.6 %collective-permute-start.24 = (f32[8,1024]{1,0:T(8,128)S(1)}, f32[8,1024]{1,0:T(8,128)S(1)}, u32[]{:S(2)}, u32[]{:S(2)}) collective-permute-start(f32[8,1024]{1,0:T(8,128)S(1)} %fusion), channel_id=1, source_target_pairs={{0,100},{4,104},{8,108},{12,112},{16,116},{20,120},{24,124},{28,12... | collective-permute-start | bytes 98312
  676.0 21.7 %collective-permute-start.23 = (f32[8,1024]{1,0:T(8,128)S(1)}, f32[8,1024]{1,0:T(8,128)S(1)}, u32[]{:S(2)}, u32[]{:S(2)}) collective-permute-start(f32[8,1024]{1,0:T(8,128)S(1)} %fusion), channel_id=1, source_target_pairs={{0,96},{4,100},{8,104},{12,108},{16,112},{20,116},{24,120},{28,124... | collective-permute-start | bytes 98312
  677.3 21.7 %collective-permute-start.22 = (f32[8,1024]{1,0:T(8,128)S(1)}, f32[8,1024]{1,0:T(8,128)S(1)}, u32[]{:S(2)}, u32[]{:S(2)}) collective-permute-start(f32[8,1024]{1,0:T(8,128)S(1)} %fusion), channel_id=1, source_target_pairs={{0,92},{4,96},{8,100},{12,104},{16,108},{20,112},{24,116},{28,120}... | collective-permute-start | bytes 98312
  686.1 15.9 %collective-permute-start.21 = (f32[8,1024]{1,0:T(8,128)S(1)}, f32[8,1024]{1,0:T(8,128)S(1)}, u32[]{:S(2)}, u32[]{:S(2)}) collective-permute-start(f32[8,1024]{1,0:T(8,128)S(1)} %fusion), channel_id=1, source_target_pairs={{0,88},{4,92},{8,96},{12,100},{16,104},{20,108},{24,112},{28,116},... | collective-permute-start | bytes 98312
  693.0 14.5 %collective-permute-start.20 = (f32[8,1024]{1,0:T(8,128)S(1)}, f32[8,1024]{1,0:T(8,128)S(1)}, u32[]{:S(2)}, u32[]{:S(2)}) collective-permute-start(f32[8,1024]{1,0:T(8,128)S(1)} %fusion), channel_id=1, source_target_pairs={{0,84},{4,88},{8,92},{12,96},{16,100},{20,104},{24,108},{28,112},{... | collective-permute-start | bytes 98312
  695.2 15.6 %collective-permute-start.19 = (f32[8,1024]{1,0:T(8,128)S(1)}, f32[8,1024]{1,0:T(8,128)S(1)}, u32[]{:S(2)}, u32[]{:S(2)}) collective-permute-start(f32[8,1024]{1,0:T(8,128)S(1)} %fusion), channel_id=1, source_target_pairs={{0,80},{4,84},{8,88},{12,92},{16,96},{20,100},{24,104},{28,108},{3... | collective-permute-start | bytes 98312
  697.7 14.9 %collective-permute-start.18 = (f32[8,1024]{1,0:T(8,128)S(1)}, f32[8,1024]{1,0:T(8,128)S(1)}, u32[]{:S(2)}, u32[]{:S(2)}) collective-permute-start(f32[8,1024]{1,0:T(8,128)S(1)} %fusion), channel_id=1, source_target_pairs={{0,76},{4,80},{8,84},{12,88},{16,92},{20,96},{24,100},{28,104},{32... | collective-permute-start | bytes 98312
  699.0 15.6 %collective-permute-start.17 = (f32[8,1024]{1,0:T(8,128)S(1)}, f32[8,1024]{1,0:T(8,128)S(1)}, u32[]{:S(2)}, u32[]{:S(2)}) collective-permute-start(f32[8,1024]{1,0:T(8,128)S(1)} %fusion), channel_id=1, source_target_pairs={{0,72},{4,76},{8,80},{12,84},{16,88},{20,92},{24,96},{28,100},{32,... | collective-permute-start | bytes 98312
  702.0 16.2 %collective-permute-start.16 = (f32[8,1024]{1,0:T(8,128)S(1)}, f32[8,1024]{1,0:T(8,128)S(1)}, u32[]{:S(2)}, u32[]{:S(2)}) collective-permute-start(f32[8,1024]{1,0:T(8,128)S(1)} %fusion), channel_id=1, source_target_pairs={{0,68},{4,72},{8,76},{12,80},{16,84},{20,88},{24,92},{28,96},{32,1... | collective-permute-start | bytes 98312
  707.5 14.5 %collective-permute-start.15 = (f32[8,1024]{1,0:T(8,128)S(1)}, f32[8,1024]{1,0:T(8,128)S(1)}, u32[]{:S(2)}, u32[]{:S(2)}) collective-permute-start(f32[8,1024]{1,0:T(8,128)S(1)} %fusion), channel_id=1, source_target_pairs={{0,64},{4,68},{8,72},{12,76},{16,80},{20,84},{24,88},{28,92},{32,9... | collective-permute-start | bytes 98312
  710.9 13.7 %collective-permute-start.14 = (f32[8,1024]{1,0:T(8,128)S(1)}, f32[8,1024]{1,0:T(8,128)S(1)}, u32[]{:S(2)}, u32[]{:S(2)}) collective-permute-start(f32[8,1024]{1,0:T(8,128)S(1)} %fusion), channel_id=1, source_target_pairs={{0,60},{4,64},{8,68},{12,72},{16,76},{20,80},{24,84},{28,88},{32,9... | collective-permute-start | bytes 98312
  712.6 15.3 %collective-permute-start.13 = (f32[8,1024]{1,0:T(8,128)S(1)}, f32[8,1024]{1,0:T(8,128)S(1)}, u32[]{:S(2)}, u32[]{:S(2)}) collective-permute-start(f32[8,1024]{1,0:T(8,128)S(1)} %fusion), channel_id=1, source_target_pairs={{0,56},{4,60},{8,64},{12,68},{16,72},{20,76},{24,80},{28,84},{32,8... | collective-permute-start | bytes 98312
  714.7 16.1 %collective-permute-start.12 = (f32[8,1024]{1,0:T(8,128)S(1)}, f32[8,1024]{1,0:T(8,128)S(1)}, u32[]{:S(2)}, u32[]{:S(2)}) collective-permute-start(f32[8,1024]{1,0:T(8,128)S(1)} %fusion), channel_id=1, source_target_pairs={{0,52},{4,56},{8,60},{12,64},{16,68},{20,72},{24,76},{28,80},{32,8... | collective-permute-start | bytes 98312
  718.2 14.8 %collective-permute-start.11 = (f32[8,1024]{1,0:T(8,128)S(1)}, f32[8,1024]{1,0:T(8,128)S(1)}, u32[]{:S(2)}, u32[]{:S(2)}) collective-permute-start(f32[8,1024]{1,0:T(8,128)S(1)} %fusion), channel_id=1, source_target_pairs={{0,48},{4,52},{8,56},{12,60},{16,64},{20,68},{24,72},{28,76},{32,8... | collective-permute-start | bytes 98312
  722.0 13.8 %collective-permute-start.10 = (f32[8,1024]{1,0:T(8,128)S(1)}, f32[8,1024]{1,0:T(8,128)S(1)}, u32[]{:S(2)}, u32[]{:S(2)}) collective-permute-start(f32[8,1024]{1,0:T(8,128)S(1)} %fusion), channel_id=1, source_target_pairs={{0,44},{4,48},{8,52},{12,56},{16,60},{20,64},{24,68},{28,72},{32,7... | collective-permute-start | bytes 98312
  724.6 19.2 %collective-permute-start.9 = (f32[8,1024]{1,0:T(8,128)S(1)}, f32[8,1024]{1,0:T(8,128)}, u32[]{:S(2)}, u32[]{:S(2)}) collective-permute-start(f32[8,1024]{1,0:T(8,128)S(1)} %fusion), channel_id=1, source_target_pairs={{0,40},{4,44},{8,48},{12,52},{16,56},{20,60},{24,64},{28,68},{32,7... | collective-permute-start | bytes 98312
  728.0 18.3 %collective-permute-start.8 = (f32[8,1024]{1,0:T(8,128)S(1)}, f32[8,1024]{1,0:T(8,128)}, u32[]{:S(2)}, u32[]{:S(2)}) collective-permute-start(f32[8,1024]{1,0:T(8,128)S(1)} %fusion), channel_id=1, source_target_pairs={{0,36},{4,40},{8,44},{12,48},{16,52},{20,56},{24,60},{28,64},{32,6... | collective-permute-start | bytes 98312
  730.8 17.9 %collective-permute-start.7 = (f32[8,1024]{1,0:T(8,128)S(1)}, f32[8,1024]{1,0:T(8,128)}, u32[]{:S(2)}, u32[]{:S(2)}) collective-permute-start(f32[8,1024]{1,0:T(8,128)S(1)} %fusion), channel_id=1, source_target_pairs={{0,32},{4,36},{8,40},{12,44},{16,48},{20,52},{24,56},{28,60},{32,6... | collective-permute-start | bytes 98312
  733.0 20.1 %collective-permute-start.6 = (f32[8,1024]{1,0:T(8,128)S(1)}, f32[8,1024]{1,0:T(8,128)}, u32[]{:S(2)}, u32[]{:S(2)}) collective-permute-start(f32[8,1024]{1,0:T(8,128)S(1)} %fusion), channel_id=1, source_target_pairs={{0,28},{4,32},{8,36},{12,40},{16,44},{20,48},{24,52},{28,56},{32,6... | collective-permute-start | bytes 98312
  736.6 19.6 %collective-permute-start.5 = (f32[8,1024]{1,0:T(8,128)S(1)}, f32[8,1024]{1,0:T(8,128)}, u32[]{:S(2)}, u32[]{:S(2)}) collective-permute-start(f32[8,1024]{1,0:T(8,128)S(1)} %fusion), channel_id=1, source_target_pairs={{0,24},{4,28},{8,32},{12,36},{16,40},{20,44},{24,48},{28,52},{32,5... | collective-permute-start | bytes 98312
  743.8 16.7 %collective-permute-start.4 = (f32[8,1024]{1,0:T(8,128)S(1)}, f32[8,1024]{1,0:T(8,128)S(1)}, u32[]{:S(2)}, u32[]{:S(2)}) collective-permute-start(f32[8,1024]{1,0:T(8,128)S(1)} %fusion), channel_id=1, source_target_pairs={{0,20},{4,24},{8,28},{12,32},{16,36},{20,40},{24,44},{28,48},{32,5... | collective-permute-start | bytes 98312
  746.3 14.2 %collective-permute-start.3 = (f32[8,1024]{1,0:T(8,128)S(1)}, f32[8,1024]{1,0:T(8,128)S(1)}, u32[]{:S(2)}, u32[]{:S(2)}) collective-permute-start(f32[8,1024]{1,0:T(8,128)S(1)} %fusion), channel_id=1, source_target_pairs={{0,16},{4,20},{8,24},{12,28},{16,32},{20,36},{24,40},{28,44},{32,4... | collective-permute-start | bytes 98312
  748.7 11.8 %collective-permute-start.2 = (f32[8,1024]{1,0:T(8,128)S(1)}, f32[8,1024]{1,0:T(8,128)S(1)}, u32[]{:S(2)}, u32[]{:S(2)}) collective-permute-start(f32[8,1024]{1,0:T(8,128)S(1)} %fusion), channel_id=1, source_target_pairs={{0,12},{4,16},{8,20},{12,24},{16,28},{20,32},{24,36},{28,40},{32,4... | collective-permute-start | bytes 98312
  753.1 7.3 collective-permute-start.1
  (43 other events, 1096.6 us)
Sparse Core Ops, SparseCore 0:
  203.1 53.9 all-reduce.3
